TPU v7x, 256 devices: a whole 4x4x8 slice. The times are simulated.
256 devices in a mesh: pitch: 64 (over x_lo, z, y), span: 4 (over x_hi, core).
Axes of the slice: x: 4 (x_hi: 2, x_lo: 2; x = x_hi * 2 + x_lo), y: 4, z: 8, core: 2. Of those that a mesh axis runs over, the one named last changes fastest.
Arguments:
- stator_adj: float32 [5, 64, 256, 512], P(None, 'pitch', None, 'span'), may hold values from -6 to 6
- rotor_adj: float32 [5, 64, 256, 512], P(None, 'pitch', None, 'span'), may hold values from -6 to 6
- stator_rhs: float32 [5, 64, 256, 512], P(None, 'pitch', None, 'span'), may hold values from -6 to 6
- rotor_rhs: float32 [5, 64, 256, 512], P(None, 'pitch', None, 'span'), may hold values from -6 to 6
- stator_dtau: float32 [64, 256, 512], P('pitch', None, 'span'), may hold values from 0.05 to 0.5
- rotor_dtau: float32 [64, 256, 512], P('pitch', None, 'span'), may hold values from 0.05 to 0.5
- roe_jac: bfloat16 [5, 5, 64, 256, 512], P(None, None, 'pitch', None, 'span'), may hold values from -2.5 to 2.5
- pair_index: int32 [2, 64, 256], P(None, 'pitch'), may hold values from 0 to 511
- pair_weight: float32 [2, 64, 256], P(None, 'pitch'), may hold values from 0.1 to 1
- rot_steps: int32 [2], replicated, may hold values from 0 to 63
Outputs:
- stator_out: float32 [5, 64, 256, 512], P(None, 'pitch', None, 'span')
- rotor_out: float32 [5, 64, 256, 512], P(None, 'pitch', None, 'span')
All inputs are finite; a program needn't handle non-finite values.
Results may differ from a plain program's by a relative error of at most 0.0003.
Values sent between devices are 32-bit elements; how exact they have to be, the bound alone decides.
A program may use at most 128 MiB of HBM per device.

v0:
```python
import functools

import jax
import jax.numpy as jnp
from jax import lax
from jax.experimental import pallas as pl
from jax.experimental.pallas import tpu as pltpu
from jax.sharding import PartitionSpec as P

COMP = 5
STEPS = 2
LANES = 4
span_coupling = 0.25
MESH = pl.DeviceIdType.MESH

HOME_PLANES, HOME_LANES = 0, 1
OUT_PLANES, OUT_LANES, BACK_LANES, BACK_PLANES = 2, 3, 4, 5
END_LANES, END_PLANES = 10, 11
EDGES = 12
STAGES = 13
FIELDS = 2 * COMP + 1


def kernel(
    planes,
    sections,
    rot_ref,
    index_ref,
    weight_ref,
    stator_ref,
    rotor_ref,
    stator_rhs_ref,
    rotor_rhs_ref,
    stator_dtau_ref,
    rotor_dtau_ref,
    jac_ref,
    stator_out,
    rotor_out,
    home_in,
    home_split,
    spread,
    state,
    rolled,
    base,
    relay,
    packed,
    pair_in,
    interp,
    flux,
    credit_out,
    credit_in,
    sums,
    sums_in,
    summed,
    end_split,
    end_in,
    end_rows,
    edge_out,
    edge_in,
    weights,
    weights_t,
    send_sem,
    recv_sem,
):
    faces = stator_ref.shape[1]
    span = stator_ref.shape[2]
    strips = planes * LANES
    quarter = faces // LANES
    halves = planes // 2
    rows = faces // planes

    me = lax.axis_index("pitch")
    section = lax.axis_index("span")
    plane, lane = me // LANES, lax.rem(me, LANES)
    other_planes = [lax.rem(plane + d, planes) for d in range(1, planes)]
    other_lanes = [lax.rem(lane + d, LANES) for d in range(1, LANES)]
    left, right = lax.rem(section + sections - 1, sections), lax.rem(section + 1, sections)

    def eight(i):
        return pl.ds(pl.multiple_of(8 * i, 8), 8)

    def copy_to(src, dst, stage, n, target):
        pltpu.make_async_remote_copy(
            src, dst, send_sem.at[stage, n], recv_sem.at[stage, n], device_id=target, device_id_type=MESH
        ).start()

    def to_planes(src, dst, stage, n):
        for p in other_planes:
            copy_to(src(p), dst, stage, n, {"pitch": p * LANES + lane})

    def to_lanes(src, dst, stage, n):
        for y in other_lanes:
            copy_to(src(y), dst, stage, n, {"pitch": plane * LANES + y})

    finish = []

    def arrived(buf, stage, n):
        pltpu.make_async_copy(buf, buf, recv_sem.at[stage, n]).wait()
        finish.append((buf, stage, n))

    barrier = pltpu.get_barrier_semaphore()
    for p in other_planes:
        pl.semaphore_signal(barrier, inc=1, device_id={"pitch": p * LANES + lane}, device_id_type=MESH)
    for y in other_lanes:
        pl.semaphore_signal(barrier, inc=1, device_id={"pitch": plane * LANES + y}, device_id_type=MESH)
    for t in (left, right):
        pl.semaphore_signal(barrier, inc=1, device_id={"span": t}, device_id_type=MESH)
    pl.semaphore_wait(barrier, planes - 1 + LANES - 1 + 2)

    def field(n):
        if n < COMP:
            return rotor_ref.at[n]
        if n < 2 * COMP:
            return rotor_rhs_ref.at[n - COMP]
        return rotor_dtau_ref

    def send_home(n):
        src = field(n)

        def part(p):
            return src.at[pl.ds(pl.multiple_of(p * rows, rows), rows)]

        to_planes(part, home_in.at[n, plane], HOME_PLANES, n)
        home_in[n, plane] = src[pl.ds(pl.multiple_of(plane * rows, rows), rows)]

    def split_home(n):
        arrived(home_in.at[n, pl.ds(0, planes - 1)], HOME_PLANES, n)

        def body(i, carry):
            one, two = home_in[n, 2 * i], home_in[n, 2 * i + 1]
            for y in range(LANES):
                home_split[n, y, eight(i)] = jnp.concatenate([one[4 * y : 4 * y + 4], two[4 * y : 4 * y + 4]], axis=0)
            return carry

        lax.fori_loop(0, halves, body, 0)
        to_lanes(lambda y: home_split.at[n, y], spread.at[n, lane], HOME_LANES, n)
        spread[n, lane] = home_split[n, lane]

    def spread_here(n):
        arrived(spread.at[n, pl.ds(0, LANES - 1)], HOME_LANES, n)

    def send_strips(step, c):
        rotation = rot_ref[step]
        places = []
        for b in range(LANES):
            offset = (b - 1 - rotation + 2 * strips) & (strips - 1)
            places.append((offset & (LANES - 1), offset >> 2))

        def body(a, carry):
            for b, (y, q) in enumerate(places):
                rolled[step, c, LANES * a + b] = state[step, c, y, (a + q) & (planes - 1)]
            return carry

        lax.fori_loop(0, planes, body, 0)
        rolled[step, c, strips] = state[step, c, places[0][0], places[0][1]]

        def part(p):
            return rolled.at[step, c, pl.ds(p * LANES, LANES + 1)]

        to_planes(part, relay.at[step, c, plane], OUT_PLANES + 4 * step, c)
        relay[step, c, plane] = rolled[step, c, pl.ds(plane * LANES, LANES + 1)]

    def first_state(c):
        def body(i, carry):
            for y in range(LANES):
                held = spread[c, y, eight(i)]
                state[0, c, y, 2 * i] = held[:4]
                state[0, c, y, 2 * i + 1] = held[4:]
            return carry

        lax.fori_loop(0, halves, body, 0)

    def pack(step, c):
        arrived(relay.at[step, c, pl.ds(0, planes - 1)], OUT_PLANES + 4 * step, c)

        def body(i, carry):
            for u in range(LANES + 1):
                packed[step, c, u, eight(i)] = jnp.concatenate(
                    [relay[step, c, 2 * i, u], relay[step, c, 2 * i + 1, u]], axis=0
                )
            return carry

        lax.fori_loop(0, halves, body, 0)
        to_lanes(
            lambda y: packed.at[step, c, pl.ds(y, 2)], pair_in.at[step, c, lane], OUT_LANES + 4 * step, c
        )
        pair_in[step, c, lane] = packed[step, c, pl.ds(lane, 2)]

    def split(x):
        high = x.astype(jnp.bfloat16)
        return high, (x - high.astype(jnp.float32)).astype(jnp.bfloat16)

    def product(table, x):
        high, low = split(x)
        total = jnp.dot(table[0], high, preferred_element_type=jnp.float32)
        total += jnp.dot(table[1], high, preferred_element_type=jnp.float32)
        return total + jnp.dot(table[0], low, preferred_element_type=jnp.float32)

    def build_weights():
        place = lax.broadcasted_iota(jnp.int32, (2 * faces, faces), 0)
        half, inner = place // faces, lax.rem(place, faces)
        y, inner = inner // quarter, lax.rem(inner, quarter)
        face = half * faces + (inner // 4) * rows + 4 * y + lax.rem(inner, 4)
        table = jnp.zeros((2 * faces, faces), jnp.float32)
        for p in range(2):
            table += jnp.where(index_ref[p : p + 1] == face, weight_ref[p : p + 1], 0.0)
        weights_t[0], weights_t[1] = split(table)
        weights[0], weights[1] = split(table.T)

    def interpolate(step, c):
        arrived(pair_in.at[step, c, pl.ds(0, LANES - 1)], OUT_LANES + 4 * step, c)
        paired = jnp.concatenate([pair_in[step, c, y, h] for h in range(2) for y in range(LANES)], axis=0)
        interp[c] = product(weights, paired)

    def flux_and_credit(step, b):
        total = jac_ref[0, b].astype(jnp.float32) * interp[0]
        for a in range(1, COMP):
            total += jac_ref[a, b].astype(jnp.float32) * interp[a]
        flux[b] = total
        credit = product(weights_t, total)
        for h in range(2):
            for y in range(LANES):
                start = h * faces + y * quarter
                credit_out[step, b, y, h] = credit[start : start + quarter]
        to_lanes(
            lambda y: credit_out.at[step, b, y], credit_in.at[step, b, lane], BACK_LANES + 4 * step, b
        )
        credit_in[step, b, lane] = credit_out[step, b, lane]

    def sum_credit(step, b):
        arrived(credit_in.at[step, b, pl.ds(0, LANES - 1)], BACK_LANES + 4 * step, b)

        def body(i, carry):
            for u in range(LANES + 1):
                if u == 0:
                    total = credit_in[step, b, 0, 0, eight(i)]
                elif u == LANES:
                    total = credit_in[step, b, LANES - 1, 1, eight(i)]
                else:
                    total = credit_in[step, b, u, 0, eight(i)] + credit_in[step, b, u - 1, 1, eight(i)]
                sums[step, b, 2 * i, u] = total[:4]
                sums[step, b, 2 * i + 1, u] = total[4:]
            return carry

        lax.fori_loop(0, halves, body, 0)
        to_planes(lambda p: sums.at[step, b, p], sums_in.at[step, b, plane], BACK_PLANES + 4 * step, b)
        sums_in[step, b, plane] = sums[step, b, plane]

    def update(step, b):
        rotation = rot_ref[step]
        arrived(sums_in.at[step, b, pl.ds(0, planes - 1)], BACK_PLANES + 4 * step, b)

        def gather(p, carry):
            for v in range(LANES - 1):
                summed[v, p] = sums_in[step, b, p, v + 1]
            after = (p + 1) & (planes - 1)
            summed[LANES - 1, p] = sums_in[step, b, p, LANES] + sums_in[step, b, after, 0]
            return carry

        lax.fori_loop(0, planes, gather, 0)
        places = []
        for y in range(LANES):
            offset = (y + rotation) & (strips - 1)
            places.append((offset & (LANES - 1), offset >> 2))

        def body(i, carry):
            for y, (v, q) in enumerate(places):
                first, second = (q + 2 * i) & (planes - 1), (q + 2 * i + 1) & (planes - 1)
                returned = jnp.concatenate([summed[v, first], summed[v, second]], axis=0)
                new = base[step, b, y, eight(i)] + spread[2 * COMP, y, eight(i)] * returned
                if step == 0:
                    state[1, b, y, 2 * i] = new[:4]
                    state[1, b, y, 2 * i + 1] = new[4:]
                    spread[b, y, eight(i)] = new
                else:
                    end_split[b, y, eight(i)] = new
            return carry

        lax.fori_loop(0, halves, body, 0)

    def send_edges(n, fetch):
        row = lax.broadcasted_iota(jnp.int32, (8, span), 0)
        col = lax.broadcasted_iota(jnp.int32, (8, span), 1)
        pick = ((row == 0) & (col == 0)) | ((row == 1) & (col == span - 1))
        pick = jnp.where(pick, 1.0, 0.0).astype(jnp.float32)
        for c in range(COMP):
            edge_out[n, c] = lax.dot_general(
                pick, fetch(c), (((1,), (1,)), ((), ())),
                precision=lax.Precision.HIGHEST, preferred_element_type=jnp.float32,
            )
        copy_to(edge_out.at[n], edge_in.at[n, 0], EDGES, 2 * n, {"span": right})
        copy_to(edge_out.at[n], edge_in.at[n, 1], EDGES, 2 * n + 1, {"span": left})

    def edges_here(n):
        arrived(edge_in.at[n, 0], EDGES, 2 * n)
        arrived(edge_in.at[n, 1], EDGES, 2 * n + 1)

    def laplace(n, c, x):
        row = lax.broadcasted_iota(jnp.int32, (16, span), 0)
        col = lax.broadcasted_iota(jnp.int32, (16, span), 1)
        place = ((row == 1) & (col == 0) & (section > 0)) | (
            (row == 8) & (col == span - 1) & (section < sections - 1)
        )
        place = jnp.where(place, 1.0, 0.0).astype(jnp.float32)
        held = jnp.concatenate([edge_in[n, 0, c], edge_in[n, 1, c]], axis=0)
        beyond = lax.dot_general(
            held, place, (((0,), (0,)), ((), ())),
            precision=lax.Precision.HIGHEST, preferred_element_type=jnp.float32,
        )
        at = lax.broadcasted_iota(jnp.int32, x.shape, 1)
        before = jnp.where(at == 0, 0.0, pltpu.roll(x, 1, 1))
        after = jnp.where(at == span - 1, 0.0, pltpu.roll(x, span - 1, 1))
        return before + after + beyond - 2.0 * x

    def spread_field(n):
        return spread[n].reshape(faces, span)

    def build_base(step, c):
        x = spread_field(c)
        change = spread_field(COMP + c) - x + span_coupling * laplace(1 + step, c, x)
        base[step, c] = (x + spread_field(2 * COMP) * change).reshape(LANES, quarter, span)

    def stator_step(step, c):
        source = stator_ref if step == 0 else stator_out
        x = source[c]
        change = stator_rhs_ref[c] - x + span_coupling * laplace(3 * step, c, x) - flux[c]
        stator_out[c] = x + stator_dtau_ref[...] * change

    def send_end(c):
        to_lanes(lambda y: end_split.at[c, y], end_in.at[c, lane], END_LANES, c)
        end_in[c, lane] = end_split[c, lane]

    def join_end(c):
        arrived(end_in.at[c, pl.ds(0, LANES - 1)], END_LANES, c)

        def body(i, carry):
            held = [end_in[c, y, eight(i)] for y in range(LANES)]
            end_rows[c, 2 * i] = jnp.concatenate([h[:4] for h in held], axis=0)
            end_rows[c, 2 * i + 1] = jnp.concatenate([h[4:] for h in held], axis=0)
            return carry

        lax.fori_loop(0, halves, body, 0)
        mine = pl.ds(pl.multiple_of(plane * rows, rows), rows)
        to_planes(lambda p: end_rows.at[c, p], rotor_out.at[c, mine], END_PLANES, c)
        rotor_out[c, mine] = end_rows[c, plane]

    every = range(COMP)
    for c in every:
        send_home(c)
    send_edges(0, lambda c: stator_ref[c])
    build_weights()

    def take(c):
        spread_here(c)
        first_state(c)
        send_strips(0, c)

    for c in every:
        split_home(c)
        if c:
            take(c - 1)
    take(COMP - 1)
    send_edges(1, spread_field)
    for c in every:
        pack(0, c)
        if c:
            interpolate(0, c - 1)
    for n in [2 * COMP] + list(range(COMP, 2 * COMP)):
        send_home(n)
    interpolate(0, COMP - 1)
    for b in every:
        flux_and_credit(0, b)
    edges_here(0)
    for n in [2 * COMP] + list(range(COMP, 2 * COMP)):
        split_home(n)
    for b in every:
        sum_credit(0, b)
    for c in every:
        stator_step(0, c)
    send_edges(3, lambda c: stator_out[c])
    edges_here(1)
    spread_here(2 * COMP)
    for b in every:
        spread_here(COMP + b)
        build_base(0, b)
        update(0, b)
        send_strips(1, b)
    send_edges(2, spread_field)
    for c in every:
        pack(1, c)
        if c:
            interpolate(1, c - 1)
    interpolate(1, COMP - 1)
    for b in every:
        flux_and_credit(1, b)
    edges_here(2)
    for c in every:
        build_base(1, c)
    for b in every:
        sum_credit(1, b)
    edges_here(3)
    for c in every:
        stator_step(1, c)
    for b in every:
        update(1, b)
        send_end(b)
        if b:
            join_end(b - 1)
    join_end(COMP - 1)
    for c in every:
        arrived(rotor_out.at[c, pl.ds(0, (planes - 1) * rows)], END_PLANES, c)
    for buf, stage, n in finish:
        pltpu.make_async_copy(buf, buf, send_sem.at[stage, n]).wait()


def shards(
    stator_adj,
    rotor_adj,
    stator_rhs,
    rotor_rhs,
    stator_dtau,
    rotor_dtau,
    roe_jac,
    pair_index,
    pair_weight,
    rot_steps,
):
    _, _, faces, span = stator_adj.shape
    planes = lax.axis_size("pitch") // LANES
    sections = lax.axis_size("span")
    quarter, rows = faces // LANES, faces // planes
    f32, bf16 = jnp.float32, jnp.bfloat16
    vmem = pl.BlockSpec(memory_space=pltpu.VMEM)
    out = jax.ShapeDtypeStruct((COMP, faces, span), f32)
    strips = planes * LANES
    scratch = [
        pltpu.VMEM((FIELDS, planes, rows, span), f32),
        pltpu.VMEM((FIELDS, LANES, quarter, span), f32),
        pltpu.VMEM((FIELDS, LANES, quarter, span), f32),
        pltpu.VMEM((STEPS, COMP, LANES, planes, 4, span), f32),
        pltpu.VMEM((STEPS, COMP, strips + 1, 4, span), f32),
        pltpu.VMEM((STEPS, COMP, LANES, quarter, span), f32),
        pltpu.VMEM((STEPS, COMP, planes, LANES + 1, 4, span), f32),
        pltpu.VMEM((STEPS, COMP, LANES + 1, quarter, span), f32),
        pltpu.VMEM((STEPS, COMP, LANES, 2, quarter, span), f32),
        pltpu.VMEM((COMP, faces, span), f32),
        pltpu.VMEM((COMP, faces, span), f32),
        pltpu.VMEM((STEPS, COMP, LANES, 2, quarter, span), f32),
        pltpu.VMEM((STEPS, COMP, LANES, 2, quarter, span), f32),
        pltpu.VMEM((STEPS, COMP, planes, LANES + 1, 4, span), f32),
        pltpu.VMEM((STEPS, COMP, planes, LANES + 1, 4, span), f32),
        pltpu.VMEM((LANES, planes, 4, span), f32),
        pltpu.VMEM((COMP, LANES, quarter, span), f32),
        pltpu.VMEM((COMP, LANES, quarter, span), f32),
        pltpu.VMEM((COMP, planes, rows, span), f32),
        pltpu.VMEM((4, COMP, 8, faces), f32),
        pltpu.VMEM((4, 2, COMP, 8, faces), f32),
        pltpu.VMEM((2, faces, 2 * faces), bf16),
        pltpu.VMEM((2, 2 * faces, faces), bf16),
        pltpu.SemaphoreType.DMA((STAGES, FIELDS)),
        pltpu.SemaphoreType.DMA((STAGES, FIELDS)),
    ]
    stator, rotor = pl.pallas_call(
        functools.partial(kernel, planes, sections),
        out_shape=(out, out),
        in_specs=[pl.BlockSpec(memory_space=pltpu.SMEM)] + [vmem] * 9,
        out_specs=(vmem, vmem),
        scratch_shapes=scratch,
        compiler_params=pltpu.CompilerParams(
            collective_id=0, has_side_effects=True, vmem_limit_bytes=60 * 1024 * 1024
        ),
        name="sliding_interface",
    )(
        rot_steps,
        pair_index[:, 0],
        pair_weight[:, 0],
        stator_adj[:, 0],
        rotor_adj[:, 0],
        stator_rhs[:, 0],
        rotor_rhs[:, 0],
        stator_dtau[0],
        rotor_dtau[0],
        roe_jac[:, :, 0],
    )
    return stator[:, None], rotor[:, None]


def solution(mesh):
    in_specs = (
        P(None, "pitch", None, "span"),
        P(None, "pitch", None, "span"),
        P(None, "pitch", None, "span"),
        P(None, "pitch", None, "span"),
        P("pitch", None, "span"),
        P("pitch", None, "span"),
        P(None, None, "pitch", None, "span"),
        P(None, "pitch", None),
        P(None, "pitch", None),
        P(),
    )
    out_specs = (P(None, "pitch", None, "span"), P(None, "pitch", None, "span"))
    return jax.shard_map(shards, mesh=mesh, in_specs=in_specs, out_specs=out_specs, check_vma=False)
```

profile of v0, /device:TPU:32, one launch (start us, length us, event | category | flops | bytes accessed | tf_op | source)
XLA Modules:
  0.0 158.0 jit_solution(5576708680030105078)
XLA Ops:
  0.6 1.3 copy.19
  1.9 1.3 copy.18
  3.2 151.9 %sliding_interface.1 = (f32[5,256,128]{2,1,0:T(8,128)}, f32[5,256,128]{2,1,0:T(8,128)}) custom-call(s32[2]{0:T(128)} %rot_ref.1, s32[2,256]{1,0:T(2,128)} %bitcast.28, f32[2,256]{1,0:T(2,128)} %bitcast.29, f32[5,256,128]{2,1,0:T(8,128)} %bitcast.22, f32[5,256,128]{2,1,0:T(8,128)} %bitcast.23, f32[5,256,128]{2,1,0:T(8,128)} %bitcast.24, ...), custom_call_target="tpu_custom_call" | custom-call | tf_op jit(solution)/shard_map/sliding_interface/pallas_call | solution.py:463
  155.1 0.0 copy-start
  155.1 2.0 %copy.22 = f32[5,1,256,128]{3,2,1,0:T(8,128)} copy(f32[5,1,256,128]{3,2,1,0:T(8,128)} %bitcast.21) | data formatting | bytes 1310720
  157.1 0.0 copy-done
  157.1 0.8 copy.23
Async XLA Ops:
  155.1 2.0 %copy-start = (f32[5,256,128]{2,1,0:T(8,128)S(1)}, f32[5,256,128]{2,1,0:T(8,128)}, u32[]{:S(2)}) copy-start(f32[5,256,128]{2,1,0:T(8,128)} %get-tuple-element.5) | copy-start | bytes 1966084
where the time goes:
time: 159 us; the launch traced here: 158 us
  Pallas kernels  152 us (96%)
  local copies, waits for them, and re-layouts  5.39 us (3%)
    pallas_call x1, Pallas kernels, shards(): pl.pallas_call(functools.partial(kernel, planes, sections), out_shape=(ou...  152 us
    unnamed x6, local copies, waits for them, and re-layouts  5.39 us

commit v1 on v0

--- a/solution.py
+++ b/solution.py
@@ -17,7 +17,8 @@
 OUT_PLANES, OUT_LANES, BACK_LANES, BACK_PLANES = 2, 3, 4, 5
 END_LANES, END_PLANES = 10, 11
 EDGES = 12
-STAGES = 13
+LOCAL = 13
+STAGES = 14
 FIELDS = 2 * COMP + 1
 
 
@@ -27,15 +28,19 @@
     rot_ref,
     index_ref,
     weight_ref,
-    stator_ref,
-    rotor_ref,
-    stator_rhs_ref,
-    rotor_rhs_ref,
-    stator_dtau_ref,
-    rotor_dtau_ref,
-    jac_ref,
+    stator_hbm,
+    rotor_hbm,
+    stator_rhs_hbm,
+    rotor_rhs_hbm,
+    stator_dtau_hbm,
+    rotor_dtau_hbm,
+    jac_hbm,
     stator_out,
     rotor_out,
+    stator_ref,
+    stator_rhs_ref,
+    stator_dtau_ref,
+    jac_ref,
     home_in,
     home_split,
     spread,
@@ -62,8 +67,7 @@
     send_sem,
     recv_sem,
 ):
-    faces = stator_ref.shape[1]
-    span = stator_ref.shape[2]
+    faces, span = stator_ref.shape[1:]
     strips = planes * LANES
     quarter = faces // LANES
     halves = planes // 2
@@ -94,9 +98,27 @@
 
     finish = []
 
+    def wait(buf, stage, n):
+        pltpu.make_async_copy(buf, buf, recv_sem.at[stage, n]).wait()
+
     def arrived(buf, stage, n):
-        pltpu.make_async_copy(buf, buf, recv_sem.at[stage, n]).wait()
+        wait(buf, stage, n)
         finish.append((buf, stage, n))
+
+    def keep(src, dst, stage, n):
+        pltpu.make_async_copy(src, dst, recv_sem.at[stage, n]).start()
+
+    own = (
+        (stator_hbm, stator_ref),
+        (stator_dtau_hbm, stator_dtau_ref),
+        (stator_rhs_hbm, stator_rhs_ref),
+        (jac_hbm, jac_ref),
+    )
+    for n, (src, dst) in enumerate(own):
+        keep(src, dst, LOCAL, n)
+
+    def own_here(n):
+        wait(own[n][1], LOCAL, n)
 
     barrier = pltpu.get_barrier_semaphore()
     for p in other_planes:
@@ -109,10 +131,10 @@
 
     def field(n):
         if n < COMP:
-            return rotor_ref.at[n]
+            return rotor_hbm.at[n]
         if n < 2 * COMP:
-            return rotor_rhs_ref.at[n - COMP]
-        return rotor_dtau_ref
+            return rotor_rhs_hbm.at[n - COMP]
+        return rotor_dtau_hbm
 
     def send_home(n):
         src = field(n)
@@ -121,10 +143,11 @@
             return src.at[pl.ds(pl.multiple_of(p * rows, rows), rows)]
 
         to_planes(part, home_in.at[n, plane], HOME_PLANES, n)
-        home_in[n, plane] = src[pl.ds(pl.multiple_of(plane * rows, rows), rows)]
+        keep(part(plane), home_in.at[n, plane], HOME_PLANES, n)
 
     def split_home(n):
-        arrived(home_in.at[n, pl.ds(0, planes - 1)], HOME_PLANES, n)
+        wait(home_in.at[n], HOME_PLANES, n)
+        finish.append((home_in.at[n, pl.ds(0, planes - 1)], HOME_PLANES, n))
 
         def body(i, carry):
             one, two = home_in[n, 2 * i], home_in[n, 2 * i + 1]
@@ -203,19 +226,22 @@
         face = half * faces + (inner // 4) * rows + 4 * y + lax.rem(inner, 4)
         table = jnp.zeros((2 * faces, faces), jnp.float32)
         for p in range(2):
-            table += jnp.where(index_ref[p : p + 1] == face, weight_ref[p : p + 1], 0.0)
+            table += jnp.where(index_ref[p] == face, weight_ref[p], 0.0)
         weights_t[0], weights_t[1] = split(table)
         weights[0], weights[1] = split(table.T)
 
     def interpolate(step, c):
         arrived(pair_in.at[step, c, pl.ds(0, LANES - 1)], OUT_LANES + 4 * step, c)
         paired = jnp.concatenate([pair_in[step, c, y, h] for h in range(2) for y in range(LANES)], axis=0)
-        interp[c] = product(weights, paired)
+        value = product(weights, paired)
+        interp[c] = value
+        if c < COMP - 1:
+            for b in range(COMP):
+                term = jac_ref[c, b].astype(jnp.float32) * value
+                flux[b] = flux[b] + term if c else term
 
     def flux_and_credit(step, b):
-        total = jac_ref[0, b].astype(jnp.float32) * interp[0]
-        for a in range(1, COMP):
-            total += jac_ref[a, b].astype(jnp.float32) * interp[a]
+        total = flux[b] + jac_ref[COMP - 1, b].astype(jnp.float32) * interp[COMP - 1]
         flux[b] = total
         credit = product(weights_t, total)
         for h in range(2):
@@ -342,65 +368,74 @@
         lax.fori_loop(0, halves, body, 0)
         mine = pl.ds(pl.multiple_of(plane * rows, rows), rows)
         to_planes(lambda p: end_rows.at[c, p], rotor_out.at[c, mine], END_PLANES, c)
-        rotor_out[c, mine] = end_rows[c, plane]
+        keep(end_rows.at[c, plane], rotor_out.at[c, mine], END_PLANES, c)
 
     every = range(COMP)
-    for c in every:
-        send_home(c)
-    send_edges(0, lambda c: stator_ref[c])
-    build_weights()
+    late = [2 * COMP] + [COMP + c for c in every]
 
     def take(c):
         spread_here(c)
         first_state(c)
         send_strips(0, c)
 
+    def to_stator(step):
+        for c in every:
+            pack(step, c)
+            if c:
+                interpolate(step, c - 1)
+            if c == COMP - 1 and step == 0:
+                for n in late[2:]:
+                    send_home(n)
+        interpolate(step, COMP - 1)
+
+    def to_spread(step):
+        for b in every:
+            flux_and_credit(step, b)
+            if b >= 2:
+                sum_credit(step, b - 2)
+        sum_credit(step, COMP - 2)
+        sum_credit(step, COMP - 1)
+
+    for c in every:
+        send_home(c)
+    own_here(0)
+    send_edges(0, lambda c: stator_ref[c])
+    build_weights()
     for c in every:
         split_home(c)
+        if c < 2:
+            send_home(late[c])
         if c:
             take(c - 1)
     take(COMP - 1)
     send_edges(1, spread_field)
-    for c in every:
-        pack(0, c)
-        if c:
-            interpolate(0, c - 1)
-    for n in [2 * COMP] + list(range(COMP, 2 * COMP)):
-        send_home(n)
-    interpolate(0, COMP - 1)
-    for b in every:
-        flux_and_credit(0, b)
+    own_here(3)
+    to_stator(0)
+    to_spread(0)
     edges_here(0)
-    for n in [2 * COMP] + list(range(COMP, 2 * COMP)):
+    own_here(1)
+    own_here(2)
+    for n in late[:2]:
         split_home(n)
-    for b in every:
-        sum_credit(0, b)
     for c in every:
         stator_step(0, c)
     send_edges(3, lambda c: stator_out[c])
     edges_here(1)
     spread_here(2 * COMP)
     for b in every:
+        if b < COMP - 1:
+            split_home(late[b + 2])
         spread_here(COMP + b)
         build_base(0, b)
         update(0, b)
         send_strips(1, b)
     send_edges(2, spread_field)
-    for c in every:
-        pack(1, c)
-        if c:
-            interpolate(1, c - 1)
-    interpolate(1, COMP - 1)
-    for b in every:
-        flux_and_credit(1, b)
+    to_stator(1)
+    to_spread(1)
     edges_here(2)
     for c in every:
         build_base(1, c)
-    for b in every:
-        sum_credit(1, b)
     edges_here(3)
-    for c in every:
-        stator_step(1, c)
     for b in every:
         update(1, b)
         send_end(b)
@@ -408,7 +443,10 @@
             join_end(b - 1)
     join_end(COMP - 1)
     for c in every:
-        arrived(rotor_out.at[c, pl.ds(0, (planes - 1) * rows)], END_PLANES, c)
+        stator_step(1, c)
+    for c in every:
+        wait(rotor_out.at[c], END_PLANES, c)
+        finish.append((rotor_out.at[c, pl.ds(0, (planes - 1) * rows)], END_PLANES, c))
     for buf, stage, n in finish:
         pltpu.make_async_copy(buf, buf, send_sem.at[stage, n]).wait()
 
@@ -431,9 +469,14 @@
     quarter, rows = faces // LANES, faces // planes
     f32, bf16 = jnp.float32, jnp.bfloat16
     vmem = pl.BlockSpec(memory_space=pltpu.VMEM)
-    out = jax.ShapeDtypeStruct((COMP, faces, span), f32)
+    hbm = pl.BlockSpec(memory_space=pl.ANY)
+    out = pltpu.VMEM((COMP, faces, span), f32)
     strips = planes * LANES
     scratch = [
+        pltpu.VMEM((COMP, faces, span), f32),
+        pltpu.VMEM((COMP, faces, span), f32),
+        pltpu.VMEM((faces, span), f32),
+        pltpu.VMEM((COMP, COMP, faces, span), bf16),
         pltpu.VMEM((FIELDS, planes, rows, span), f32),
         pltpu.VMEM((FIELDS, LANES, quarter, span), f32),
         pltpu.VMEM((FIELDS, LANES, quarter, span), f32),
@@ -463,7 +506,7 @@
     stator, rotor = pl.pallas_call(
         functools.partial(kernel, planes, sections),
         out_shape=(out, out),
-        in_specs=[pl.BlockSpec(memory_space=pltpu.SMEM)] + [vmem] * 9,
+        in_specs=[pl.BlockSpec(memory_space=pltpu.SMEM), vmem, vmem] + [hbm] * 7,
         out_specs=(vmem, vmem),
         scratch_shapes=scratch,
         compiler_params=pltpu.CompilerParams(
@@ -472,8 +515,8 @@
         name="sliding_interface",
     )(
         rot_steps,
-        pair_index[:, 0],
-        pair_weight[:, 0],
+        pair_index,
+        pair_weight,
         stator_adj[:, 0],
         rotor_adj[:, 0],
         stator_rhs[:, 0],

time: 159 us -> 154 us (0.969)
  local copies, waits for them, and re-layouts: 5.39 us -> 1.67 us
    unnamed x6 -> x2, local copies, waits for them, and re-layouts: 5.39 us -> 1.67 us
where the time goes in v1:
time: 154 us
  Pallas kernels  151 us (98%)
  local copies, waits for them, and re-layouts  1.67 us (1%)
    pallas_call x1, Pallas kernels, shards(): pl.pallas_call(functools.partial(kernel, planes, sections), out_shape=(ou...  151 us

profile of v1, /device:TPU:32, one launch (start us, length us, event | category | flops | bytes accessed | tf_op | source)
XLA Modules:
  0.0 153.7 jit_solution(4754016187725481731)
XLA Ops:
  0.6 151.4 %sliding_interface.1 = (f32[5,256,128]{2,1,0:T(8,128)S(1)}, f32[5,256,128]{2,1,0:T(8,128)S(1)}) custom-call(s32[2]{0:T(128)} %rot_ref.1, s32[2,1,256]{2,1,0:T(1,128)} %index_ref.1, f32[2,1,256]{2,1,0:T(1,128)} %weight_ref.1, f32[5,256,128]{2,1,0:T(8,128)} %bitcast.16, f32[5,256,128]{2,1,0:T(8,128)} %bitcast.17, f32[5,256,128]{2,1,0:T(8,128)} %bitcast.18, ...), custom_call_target="tpu_custom_call" | custom-call | tf_op jit(solution)/shard_map/sliding_interface/pallas_call | solution.py:506
  152.0 0.8 copy.16
  152.8 0.8 copy.17

commit v2 on v1

--- a/solution.py
+++ b/solution.py
@@ -384,7 +384,7 @@
             if c:
                 interpolate(step, c - 1)
             if c == COMP - 1 and step == 0:
-                for n in late[2:]:
+                for n in late:
                     send_home(n)
         interpolate(step, COMP - 1)
 
@@ -403,8 +403,6 @@
     build_weights()
     for c in every:
         split_home(c)
-        if c < 2:
-            send_home(late[c])
         if c:
             take(c - 1)
     take(COMP - 1)

time: 154 us -> 152 us (0.987)
  Pallas kernels: 151 us -> 149 us
    pallas_call x1, Pallas kernels: 151 us -> 149 us  [shards(): pl.pallas_call(functools.partial(kernel, planes, sections), out_shape=(ou...]
where the time goes in v2:
time: 152 us; the launch traced here: 151 us
  Pallas kernels  149 us (98%)
  local copies, waits for them, and re-layouts  1.67 us (1%)
    pallas_call x1, Pallas kernels, shards(): pl.pallas_call(functools.partial(kernel, planes, sections), out_shape=(ou...  149 us

profile of v2, /device:TPU:32, one launch (start us, length us, event | category | flops | bytes accessed | tf_op | source)
XLA Modules:
  0.0 151.1 jit_solution(3735833709128854073)
XLA Ops:
  0.6 148.8 %sliding_interface.1 = (f32[5,256,128]{2,1,0:T(8,128)S(1)}, f32[5,256,128]{2,1,0:T(8,128)S(1)}) custom-call(s32[2]{0:T(128)} %rot_ref.1, s32[2,1,256]{2,1,0:T(1,128)} %index_ref.1, f32[2,1,256]{2,1,0:T(1,128)} %weight_ref.1, f32[5,256,128]{2,1,0:T(8,128)} %bitcast.16, f32[5,256,128]{2,1,0:T(8,128)} %bitcast.17, f32[5,256,128]{2,1,0:T(8,128)} %bitcast.18, ...), custom_call_target="tpu_custom_call" | custom-call | tf_op jit(solution)/shard_map/sliding_interface/pallas_call | solution.py:504
  149.4 0.8 copy.16
  150.3 0.8 copy.17

commit v3 on v2

--- a/solution.py
+++ b/solution.py
@@ -381,6 +381,8 @@
     def to_stator(step):
         for c in every:
             pack(step, c)
+            if c == (COMP - 1 if step else 2):
+                send_edges(1 + step, spread_field)
             if c:
                 interpolate(step, c - 1)
             if c == COMP - 1 and step == 0:
@@ -406,7 +408,6 @@
         if c:
             take(c - 1)
     take(COMP - 1)
-    send_edges(1, spread_field)
     own_here(3)
     to_stator(0)
     to_spread(0)
@@ -427,7 +428,6 @@
         build_base(0, b)
         update(0, b)
         send_strips(1, b)
-    send_edges(2, spread_field)
     to_stator(1)
     to_spread(1)
     edges_here(2)

time: 152 us -> 153 us (level)
  no operation moved by 1% of the time
where the time goes in v3:
time: 153 us
  Pallas kernels  150 us (98%)
  local copies, waits for them, and re-layouts  1.67 us (1%)
    pallas_call x1, Pallas kernels, shards(): pl.pallas_call(functools.partial(kernel, planes, sections), out_shape=(ou...  150 us

profile of v3, /device:TPU:32, one launch (start us, length us, event | category | flops | bytes accessed | tf_op | source)
XLA Modules:
  0.0 152.6 jit_solution(16108730944098282812)
XLA Ops:
  0.6 150.2 %sliding_interface.1 = (f32[5,256,128]{2,1,0:T(8,128)S(1)}, f32[5,256,128]{2,1,0:T(8,128)S(1)}) custom-call(s32[2]{0:T(128)} %rot_ref.1, s32[2,1,256]{2,1,0:T(1,128)} %index_ref.1, f32[2,1,256]{2,1,0:T(1,128)} %weight_ref.1, f32[5,256,128]{2,1,0:T(8,128)} %bitcast.16, f32[5,256,128]{2,1,0:T(8,128)} %bitcast.17, f32[5,256,128]{2,1,0:T(8,128)} %bitcast.18, ...), custom_call_target="tpu_custom_call" | custom-call | tf_op jit(solution)/shard_map/sliding_interface/pallas_call | solution.py:504
  150.9 0.8 copy.16
  151.7 0.8 copy.17
